TPU v7x, 32 devices: a whole 2x2x4 slice. The times are simulated.
32 devices in a mesh: dp: 4 (over z), fsdp: 8 (over y, x, core).
Axes of the slice: x: 2, y: 2, z: 4, core: 2. Of those that a mesh axis runs over, the one named last changes fastest.
Arguments:
- words_in: bfloat16 [384, 20, 768], P(('dp', 'fsdp')), may hold values from -6 to 6
- regions_in: bfloat16 [384, 36, 768], P(('dp', 'fsdp')), may hold values from -6 to 6
- word_mask: int32 [384, 20], P(('dp', 'fsdp')), may hold values from 0 to 1, as said below
- region_count: int32 [384], P(('dp', 'fsdp')), may hold values from 10 to 36, as said below
- cross_matrices: bfloat16 [4, 768, 768], P(None, 'fsdp'), may hold values from -0.3125 to 0.3125
- cross_vectors: bfloat16 [5, 768], P(None, 'fsdp'), may hold values from -1.5 to 1.5
- word_self_matrices: bfloat16 [4, 768, 768], P(None, 'fsdp'), may hold values from -0.3125 to 0.3125
- word_self_vectors: bfloat16 [5, 768], P(None, 'fsdp'), may hold values from -1.5 to 1.5
- region_self_matrices: bfloat16 [4, 768, 768], P(None, 'fsdp'), may hold values from -0.3125 to 0.3125
- region_self_vectors: bfloat16 [5, 768], P(None, 'fsdp'), may hold values from -1.5 to 1.5
- word_feed_matrices: bfloat16 [2, 768, 3072], P(None, 'fsdp'), may hold values from -0.21875 to 0.21875
- word_feed_vectors: bfloat16 [7, 768], P(None, 'fsdp'), may hold values from -1.5 to 1.5
- region_feed_matrices: bfloat16 [2, 768, 3072], P(None, 'fsdp'), may hold values from -0.21875 to 0.21875
- region_feed_vectors: bfloat16 [7, 768], P(None, 'fsdp'), may hold values from -1.5 to 1.5
- words_cotangent: bfloat16 [384, 20, 768], P(('dp', 'fsdp')), may hold values from -6 to 6
- regions_cotangent: bfloat16 [384, 36, 768], P(('dp', 'fsdp')), may hold values from -6 to 6
Outputs:
- words_out: bfloat16 [384, 20, 768], P(('dp', 'fsdp'))
- regions_out: bfloat16 [384, 36, 768], P(('dp', 'fsdp'))
- words_grad: bfloat16 [384, 20, 768], P(('dp', 'fsdp'))
- regions_grad: bfloat16 [384, 36, 768], P(('dp', 'fsdp'))
- grad_cross_matrices: float32 [4, 768, 768], P(None, 'fsdp')
- grad_cross_vectors: float32 [5, 768], P(None, 'fsdp')
- grad_word_self_matrices: float32 [4, 768, 768], P(None, 'fsdp')
- grad_word_self_vectors: float32 [5, 768], P(None, 'fsdp')
- grad_region_self_matrices: float32 [4, 768, 768], P(None, 'fsdp')
- grad_region_self_vectors: float32 [5, 768], P(None, 'fsdp')
- grad_word_feed_matrices: float32 [2, 768, 3072], P(None, 'fsdp')
- grad_word_feed_vectors: float32 [7, 768], P(None, 'fsdp')
- grad_region_feed_matrices: float32 [2, 768, 3072], P(None, 'fsdp')
- grad_region_feed_vectors: float32 [7, 768], P(None, 'fsdp')
Inputs may be any that keep to these rules, and one draw needn't show every extreme that they name: `word_mask`: position 0 of every item is 1. `region_count`: some item has exactly 36 regions.
All inputs are finite; a program needn't handle non-finite values.
Results may differ from a plain program's by a relative error of at most 0.024.
Values may be sent and summed in bfloat16 or wider, within the bound.
No kernel may reach another device: no remote copies, remote signals or barrier semaphores. Data moves between devices by JAX's collectives and lax.ppermute only.
A program may use at most 320 MiB of HBM per device.

v0:
```python
from functools import partial
import math

import jax
import jax.numpy as jnp
from jax import lax
from jax.sharding import PartitionSpec as P

HEADS = 12


epsilon = 1e-12
negative = -10000.0


def normalize(total, gain, shift):
    centred = total - jnp.mean(total, axis=-1, keepdims=True)
    spread = jnp.mean(centred * centred, axis=-1, keepdims=True)
    return centred * lax.rsqrt(spread + epsilon) * gain + shift


def normalize_back(grad_out, total, gain, shift):
    _, puller = jax.vjp(normalize, total, gain, shift)
    return puller(grad_out)


def product(left, right):
    return jnp.dot(left, right, preferred_element_type=jnp.float32)


def outer(left, right):
    return lax.dot_general(
        left, right, (((0,), (0,)), ((), ())), preferred_element_type=jnp.float32
    )


def through(grad_rows, weight):
    return lax.dot_general(
        grad_rows, weight, (((1,), (1,)), ((), ())), preferred_element_type=jnp.float32
    )


def column_sum(values):
    return jnp.sum(values.astype(jnp.float32), axis=0)


def split_heads(rows, items):
    return rows.reshape(items, -1, HEADS, rows.shape[-1] // HEADS)


def scores_of(queries, keys_low, key_bias, items):
    query_heads = split_heads(queries, items)
    key_heads = split_heads(keys_low, items)
    raw = jnp.einsum("iqhe,ikhe->ihqk", query_heads, key_heads, preferred_element_type=jnp.float32)
    return raw / math.sqrt(query_heads.shape[-1]) + key_bias[:, None, None, :]


def attend(query_rows, context_rows, key_bias, weight, terms, items):
    queries = (product(query_rows, weight[0]) + terms[0]).astype(jnp.bfloat16)
    keys_low = product(context_rows, weight[1]).astype(jnp.bfloat16)
    values_low = (product(context_rows, weight[2]) + terms[1]).astype(jnp.bfloat16)
    scores = scores_of(queries, keys_low, key_bias, items)
    largest = jnp.max(scores, axis=-1, keepdims=True)
    raised = jnp.exp(scores - largest)
    totals = jnp.sum(raised, axis=-1, keepdims=True)
    probs_low = (raised / totals).astype(jnp.bfloat16)
    mixed = jnp.einsum(
        "ihqk,ikhe->iqhe",
        probs_low,
        split_heads(values_low, items),
        preferred_element_type=jnp.float32,
    )
    context_low = mixed.reshape(query_rows.shape).astype(jnp.bfloat16)
    branch = product(context_low, weight[3]) + terms[2]
    return (branch, (queries, keys_low, values_low, largest + jnp.log(totals), context_low))


def attend_back(grad_branch, kept, query_rows, context_rows, key_bias, weight, items):
    queries, keys_low, values_low, log_totals, context_low = kept
    grad_out = grad_branch.astype(jnp.bfloat16)
    grad_output_weight = outer(context_low, grad_out)
    grad_context = through(grad_out, weight[3]).astype(jnp.bfloat16)
    probs = jnp.exp(scores_of(queries, keys_low, key_bias, items) - log_totals)
    context_heads = split_heads(grad_context, items)
    value_heads = split_heads(values_low, items)
    grad_probs = jnp.einsum(
        "iqhe,ikhe->ihqk", context_heads, value_heads, preferred_element_type=jnp.float32
    )
    grad_values = jnp.einsum(
        "ihqk,iqhe->ikhe",
        probs.astype(jnp.bfloat16),
        context_heads,
        preferred_element_type=jnp.float32,
    )
    grad_scores = (
        probs * (grad_probs - jnp.sum(probs * grad_probs, axis=-1, keepdims=True))
    ).astype(jnp.bfloat16)
    scale = math.sqrt(value_heads.shape[-1])
    grad_queries = (
        (
            jnp.einsum(
                "ihqk,ikhe->iqhe",
                grad_scores,
                split_heads(keys_low, items),
                preferred_element_type=jnp.float32,
            )
            / scale
        )
        .reshape(queries.shape)
        .astype(jnp.bfloat16)
    )
    grad_keys = (
        (
            jnp.einsum(
                "ihqk,iqhe->ikhe",
                grad_scores,
                split_heads(queries, items),
                preferred_element_type=jnp.float32,
            )
            / scale
        )
        .reshape(keys_low.shape)
        .astype(jnp.bfloat16)
    )
    grad_values_low = grad_values.reshape(values_low.shape).astype(jnp.bfloat16)
    weights_grad = jnp.stack(
        [
            outer(query_rows, grad_queries),
            outer(context_rows, grad_keys),
            outer(context_rows, grad_values_low),
            grad_output_weight,
        ]
    )
    biases_grad = jnp.stack(
        [column_sum(grad_queries), column_sum(grad_values_low), column_sum(grad_out)]
    )
    grad_query_rows = through(grad_queries, weight[0])
    grad_context_rows = through(grad_keys, weight[1]) + through(grad_values_low, weight[2])
    return (grad_query_rows, grad_context_rows, weights_grad, biases_grad)


def feed(rows_low, weight, terms):
    hidden_pre = product(rows_low, weight[0]) + terms[0:4].reshape(-1)
    hidden_low = jax.nn.gelu(hidden_pre, approximate=False).astype(jnp.bfloat16)
    branch = through(hidden_low, weight[1]) + terms[4]
    return (branch, hidden_pre, hidden_low)


def feed_back(grad_total, rows_low, hidden_pre, hidden_low, weight):
    grad_branch = grad_total.astype(jnp.bfloat16)
    grad_down = outer(grad_branch, hidden_low)
    grad_hidden = product(grad_branch, weight[1])
    _, gelu_pull = jax.vjp(partial(jax.nn.gelu, approximate=False), hidden_pre)
    grad_pre = gelu_pull(grad_hidden)[0].astype(jnp.bfloat16)
    grad_up = outer(rows_low, grad_pre)
    grad_rows = through(grad_pre, weight[0]) + grad_total
    biases_grad = jnp.concatenate(
        [column_sum(grad_pre).reshape(4, -1), column_sum(grad_branch)[None]]
    )
    return (grad_rows, jnp.stack([grad_up, grad_down]), biases_grad)


def local(
    words_in,
    regions_in,
    word_mask,
    region_count,
    cross_matrices,
    cross_vectors,
    word_self_matrices,
    word_self_vectors,
    region_self_matrices,
    region_self_vectors,
    word_feed_matrices,
    word_feed_vectors,
    region_feed_matrices,
    region_feed_vectors,
    words_cotangent,
    regions_cotangent,
):
    items, words, width = words_in.shape
    regions = regions_in.shape[1]
    word_bias = (word_mask.astype(jnp.float32) - 1.0) * 10000.0
    region_bias = jnp.where(
        jnp.arange(regions)[None, :] < region_count[:, None], 0.0, negative
    ).astype(jnp.float32)
    word_rows = words_in.reshape(-1, width)
    region_rows = regions_in.reshape(-1, width)
    cross_weight, cross_vector = (
        lax.all_gather(cross_matrices, "fsdp", axis=1, tiled=True),
        lax.all_gather(cross_vectors, "fsdp", axis=1, tiled=True),
    )
    cross_terms = cross_vector.astype(jnp.float32)
    word_branch, word_cross_kept = attend(
        word_rows, region_rows, region_bias, cross_weight, cross_terms, items
    )
    region_branch, region_cross_kept = attend(
        region_rows, word_rows, word_bias, cross_weight, cross_terms, items
    )
    word_cross_total = word_rows.astype(jnp.float32) + word_branch
    region_cross_total = region_rows.astype(jnp.float32) + region_branch
    word_cross = normalize(word_cross_total, cross_terms[3], cross_terms[4])
    region_cross = normalize(region_cross_total, cross_terms[3], cross_terms[4])
    word_cross_low = word_cross.astype(jnp.bfloat16)
    region_cross_low = region_cross.astype(jnp.bfloat16)
    self_full = (
        lax.all_gather(word_self_matrices, "fsdp", axis=1, tiled=True),
        lax.all_gather(word_self_vectors, "fsdp", axis=1, tiled=True),
        lax.all_gather(region_self_matrices, "fsdp", axis=1, tiled=True),
        lax.all_gather(region_self_vectors, "fsdp", axis=1, tiled=True),
    )
    word_self_terms = self_full[1].astype(jnp.float32)
    region_self_terms = self_full[3].astype(jnp.float32)
    word_self_branch, word_self_kept = attend(
        word_cross_low, word_cross_low, word_bias, self_full[0], word_self_terms, items
    )
    region_self_branch, region_self_kept = attend(
        region_cross_low, region_cross_low, region_bias, self_full[2], region_self_terms, items
    )
    word_self_total = word_cross + word_self_branch
    region_self_total = region_cross + region_self_branch
    word_selfed = normalize(word_self_total, word_self_terms[3], word_self_terms[4])
    region_selfed = normalize(region_self_total, region_self_terms[3], region_self_terms[4])
    word_selfed_low = word_selfed.astype(jnp.bfloat16)
    region_selfed_low = region_selfed.astype(jnp.bfloat16)
    feed_full = (
        lax.all_gather(word_feed_matrices, "fsdp", axis=1, tiled=True),
        lax.all_gather(word_feed_vectors, "fsdp", axis=1, tiled=True),
        lax.all_gather(region_feed_matrices, "fsdp", axis=1, tiled=True),
        lax.all_gather(region_feed_vectors, "fsdp", axis=1, tiled=True),
    )
    word_feed_terms = feed_full[1].astype(jnp.float32)
    region_feed_terms = feed_full[3].astype(jnp.float32)
    word_feed_branch, word_pre, word_hidden = feed(word_selfed_low, feed_full[0], word_feed_terms)
    region_feed_branch, region_pre, region_hidden = feed(
        region_selfed_low, feed_full[2], region_feed_terms
    )
    word_final_total = word_selfed + word_feed_branch
    region_final_total = region_selfed + region_feed_branch
    words_out = normalize(word_final_total, word_feed_terms[5], word_feed_terms[6])
    regions_out = normalize(region_final_total, region_feed_terms[5], region_feed_terms[6])
    feed_back_full = (
        lax.all_gather(word_feed_matrices, "fsdp", axis=1, tiled=True),
        lax.all_gather(word_feed_vectors, "fsdp", axis=1, tiled=True),
        lax.all_gather(region_feed_matrices, "fsdp", axis=1, tiled=True),
        lax.all_gather(region_feed_vectors, "fsdp", axis=1, tiled=True),
    )
    word_feed_gain = feed_back_full[1].astype(jnp.float32)
    region_feed_gain = feed_back_full[3].astype(jnp.float32)
    grad_word_final, word_gain_grad, word_shift_grad = normalize_back(
        words_cotangent.reshape(-1, width).astype(jnp.float32),
        word_final_total,
        word_feed_gain[5],
        word_feed_gain[6],
    )
    grad_region_final, region_gain_grad, region_shift_grad = normalize_back(
        regions_cotangent.reshape(-1, width).astype(jnp.float32),
        region_final_total,
        region_feed_gain[5],
        region_feed_gain[6],
    )
    grad_word_selfed, word_feed_matrix_grad, word_feed_bias_grad = feed_back(
        grad_word_final, word_selfed_low, word_pre, word_hidden, feed_back_full[0]
    )
    grad_region_selfed, region_feed_matrix_grad, region_feed_bias_grad = feed_back(
        grad_region_final, region_selfed_low, region_pre, region_hidden, feed_back_full[2]
    )
    word_feed_vector_grad = jnp.concatenate(
        [word_feed_bias_grad, word_gain_grad[None], word_shift_grad[None]]
    )
    region_feed_vector_grad = jnp.concatenate(
        [region_feed_bias_grad, region_gain_grad[None], region_shift_grad[None]]
    )
    feed_shards = (
        lax.psum_scatter(word_feed_matrix_grad, "fsdp", scatter_dimension=1, tiled=True),
        lax.psum_scatter(word_feed_vector_grad, "fsdp", scatter_dimension=1, tiled=True),
        lax.psum_scatter(region_feed_matrix_grad, "fsdp", scatter_dimension=1, tiled=True),
        lax.psum_scatter(region_feed_vector_grad, "fsdp", scatter_dimension=1, tiled=True),
    )
    self_back_full = (
        lax.all_gather(word_self_matrices, "fsdp", axis=1, tiled=True),
        lax.all_gather(word_self_vectors, "fsdp", axis=1, tiled=True),
        lax.all_gather(region_self_matrices, "fsdp", axis=1, tiled=True),
        lax.all_gather(region_self_vectors, "fsdp", axis=1, tiled=True),
    )
    word_self_gain = self_back_full[1].astype(jnp.float32)
    region_self_gain = self_back_full[3].astype(jnp.float32)
    grad_word_self_total, word_self_gain_grad, word_self_shift_grad = normalize_back(
        grad_word_selfed, word_self_total, word_self_gain[3], word_self_gain[4]
    )
    grad_region_self_total, region_self_gain_grad, region_self_shift_grad = normalize_back(
        grad_region_selfed, region_self_total, region_self_gain[3], region_self_gain[4]
    )
    word_query_grad, word_context_grad, word_self_matrix_grad, word_self_bias_grad = attend_back(
        grad_word_self_total,
        word_self_kept,
        word_cross_low,
        word_cross_low,
        word_bias,
        self_back_full[0],
        items,
    )
    region_query_grad, region_context_grad, region_self_matrix_grad, region_self_bias_grad = (
        attend_back(
            grad_region_self_total,
            region_self_kept,
            region_cross_low,
            region_cross_low,
            region_bias,
            self_back_full[2],
            items,
        )
    )
    grad_word_cross = grad_word_self_total + word_query_grad + word_context_grad
    grad_region_cross = grad_region_self_total + region_query_grad + region_context_grad
    word_self_vector_grad = jnp.concatenate(
        [word_self_bias_grad, word_self_gain_grad[None], word_self_shift_grad[None]]
    )
    region_self_vector_grad = jnp.concatenate(
        [region_self_bias_grad, region_self_gain_grad[None], region_self_shift_grad[None]]
    )
    self_shards = (
        lax.psum_scatter(word_self_matrix_grad, "fsdp", scatter_dimension=1, tiled=True),
        lax.psum_scatter(word_self_vector_grad, "fsdp", scatter_dimension=1, tiled=True),
        lax.psum_scatter(region_self_matrix_grad, "fsdp", scatter_dimension=1, tiled=True),
        lax.psum_scatter(region_self_vector_grad, "fsdp", scatter_dimension=1, tiled=True),
    )
    cross_back_weight, cross_back_vector = (
        lax.all_gather(cross_matrices, "fsdp", axis=1, tiled=True),
        lax.all_gather(cross_vectors, "fsdp", axis=1, tiled=True),
    )
    cross_gain = cross_back_vector.astype(jnp.float32)
    grad_word_total, word_cross_gain_grad, word_cross_shift_grad = normalize_back(
        grad_word_cross, word_cross_total, cross_gain[3], cross_gain[4]
    )
    grad_region_total, region_cross_gain_grad, region_cross_shift_grad = normalize_back(
        grad_region_cross, region_cross_total, cross_gain[3], cross_gain[4]
    )
    word_side_query, word_side_context, word_side_matrix, word_side_bias = attend_back(
        grad_word_total,
        word_cross_kept,
        word_rows,
        region_rows,
        region_bias,
        cross_back_weight,
        items,
    )
    region_side_query, region_side_context, region_side_matrix, region_side_bias = attend_back(
        grad_region_total,
        region_cross_kept,
        region_rows,
        word_rows,
        word_bias,
        cross_back_weight,
        items,
    )
    words_grad = grad_word_total + word_side_query + region_side_context
    regions_grad = grad_region_total + region_side_query + word_side_context
    cross_matrix_grad = word_side_matrix + region_side_matrix
    cross_vector_grad = jnp.concatenate(
        [
            word_side_bias + region_side_bias,
            (word_cross_gain_grad + region_cross_gain_grad)[None],
            (word_cross_shift_grad + region_cross_shift_grad)[None],
        ]
    )
    cross_shards = (
        lax.psum_scatter(cross_matrix_grad, "fsdp", scatter_dimension=1, tiled=True),
        lax.psum_scatter(cross_vector_grad, "fsdp", scatter_dimension=1, tiled=True),
    )
    summed = (
        lax.psum(cross_shards[0].astype(jnp.bfloat16), "dp").astype(jnp.float32),
        lax.psum(cross_shards[1].astype(jnp.bfloat16), "dp").astype(jnp.float32),
        lax.psum(self_shards[0].astype(jnp.bfloat16), "dp").astype(jnp.float32),
        lax.psum(self_shards[1].astype(jnp.bfloat16), "dp").astype(jnp.float32),
        lax.psum(self_shards[2].astype(jnp.bfloat16), "dp").astype(jnp.float32),
        lax.psum(self_shards[3].astype(jnp.bfloat16), "dp").astype(jnp.float32),
        lax.psum(feed_shards[0].astype(jnp.bfloat16), "dp").astype(jnp.float32),
        lax.psum(feed_shards[1].astype(jnp.bfloat16), "dp").astype(jnp.float32),
        lax.psum(feed_shards[2].astype(jnp.bfloat16), "dp").astype(jnp.float32),
        lax.psum(feed_shards[3].astype(jnp.bfloat16), "dp").astype(jnp.float32),
    )
    return (
        words_out.astype(jnp.bfloat16).reshape(items, words, width),
        regions_out.astype(jnp.bfloat16).reshape(items, regions, width),
        words_grad.astype(jnp.bfloat16).reshape(items, words, width),
        regions_grad.astype(jnp.bfloat16).reshape(items, regions, width),
        summed[0],
        summed[1],
        summed[2],
        summed[3],
        summed[4],
        summed[5],
        summed[6],
        summed[7],
        summed[8],
        summed[9],
    )


def solution(mesh):
    return jax.shard_map(
        local,
        mesh=mesh,
        in_specs=(
            P(("dp", "fsdp"), None, None),
            P(("dp", "fsdp"), None, None),
            P(("dp", "fsdp"), None),
            P(("dp", "fsdp")),
            P(None, "fsdp", None),
            P(None, "fsdp"),
            P(None, "fsdp", None),
            P(None, "fsdp"),
            P(None, "fsdp", None),
            P(None, "fsdp"),
            P(None, "fsdp", None),
            P(None, "fsdp"),
            P(None, "fsdp", None),
            P(None, "fsdp"),
            P(("dp", "fsdp"), None, None),
            P(("dp", "fsdp"), None, None),
        ),
        out_specs=(
            P(("dp", "fsdp"), None, None),
            P(("dp", "fsdp"), None, None),
            P(("dp", "fsdp"), None, None),
            P(("dp", "fsdp"), None, None),
            P(None, "fsdp", None),
            P(None, "fsdp"),
            P(None, "fsdp", None),
            P(None, "fsdp"),
            P(None, "fsdp", None),
            P(None, "fsdp"),
            P(None, "fsdp", None),
            P(None, "fsdp"),
            P(None, "fsdp", None),
            P(None, "fsdp"),
        ),
        check_vma=False,
    )
```

profile of v0, /device:TPU:0, one launch (start us, length us, event | category | flops | bytes accessed | tf_op | source)
XLA Modules:
  0.0 1151.0 jit_solution(7077896610551559863)
XLA Ops:
  10.7 10.4 all-gather.4
  21.8 8.9 all-gather.2
  31.5 8.1 all-gather
  39.9 8.9 all-gather.3
  51.4 7.9 all-gather.1
  85.7 6.9 all-gather.17.cloned.1.call-done
  144.4 9.0 all-gather.19.cloned.1.call-done
  153.4 17.4 %multiply_convert_fusion = (bf16[432,3072]{1,0:T(8,128)(2,1)S(1)}, f32[432,3072]{1,0:T(8,128)S(1)}, f32[432,3072]{1,0:T(8,128)}) fusion(f32[3072]{0:T(1024)S(1)} %copy-done.147, bf16[2,768,3072]{2,1,0:T(8,128)(2,1)} %all-gather.19.cloned.1.call-done, f32[432,768]{1,0:T(8,128)} %copy-done.50, f32[768]{0:T(1024)S(1)} %copy-done.162, f32[768]{0:T(1024)S(1)} %copy-done.124, ...), kind=kOutput, calls=%fused_computation.13 | convolution fusion | flops 2127679488 | bytes 19338624 | tf_op jit(solution)/shard_map/dot_general | solution.py:28
  178.0 7.3 convert_reduce_fusion
  223.6 4.9 pad_maximum_fusion.3
  260.4 10.3 multiply_convert_fusion.6
  320.4 7.0 pad_maximum_fusion.1
  332.9 7.2 pad_maximum_fusion
  427.2 5.5 maximum_add_fusion
  432.7 13.2 %copy.249 = f32[4,768,768]{2,0,1:T(4,128)} copy(f32[4,768,768]{1,2,0:T(8,128)} %maximum_add_fusion) | data formatting | bytes 18874368 | tf_op jit(solution)/shard_map/add | solution.py:359
  446.1 308.4 %all-reduce.7 = bf16[4,768,768]{2,0,1:T(4,128)(2,1)} all-reduce(f32[4,768,768]{2,0,1:T(4,128)} %copy.249), channel_id=2, replica_groups=mesh['dp'=4,'fsdp'=8] {'fsdp'}, use_global_device_ids=true, to_apply=%region_36.37.clone | all-reduce | flops 2359296 | bytes 14155776
  769.3 24.1 %reduce-scatter.24.cloned.1.call-done = f32[2,96,3072]{2,1,0:T(8,128)} async-done(((f32[2,768,3072]{2,1,0:T(8,128)}), f32[2,96,3072]{2,1,0:T(8,128)}) %reduce-scatter.24.cloned.1.call-update) | async-done | bytes 2359312 | tf_op jit(solution)/shard_map/reduce_scatter | solution.py:275
  811.9 18.3 %reduce-scatter.32.cloned.1.call-done = f32[96,5]{1,0:T(8,128)} async-done(((f32[768,5]{1,0:T(8,128)}), f32[96,5]{1,0:T(8,128)}) %reduce-scatter.32.cloned.1.call-update) | async-done | bytes 1936
  831.1 36.1 %reduce-scatter.30.cloned.1.call-done = f32[96,5]{1,0:T(8,128)} async-done(((f32[768,5]{1,0:T(8,128)}), f32[96,5]{1,0:T(8,128)}) %reduce-scatter.30.cloned.1.call-update) | async-done | bytes 1936
  868.0 35.9 %reduce-scatter.28.cloned.1.call-done = f32[96,5]{1,0:T(8,128)} async-done(((f32[768,5]{1,0:T(8,128)}), f32[96,5]{1,0:T(8,128)}) %reduce-scatter.28.cloned.1.call-update) | async-done | bytes 1936
  904.8 36.1 %reduce-scatter.36.cloned.1.call-done = f32[96,7]{1,0:T(8,128)} async-done(((f32[768,7]{1,0:T(8,128)}), f32[96,7]{1,0:T(8,128)}) %reduce-scatter.36.cloned.1.call-update) | async-done | bytes 2704
  941.7 35.9 %reduce-scatter.34.cloned.1.call-done = f32[96,7]{1,0:T(8,128)} async-done(((f32[768,7]{1,0:T(8,128)}), f32[96,7]{1,0:T(8,128)}) %reduce-scatter.34.cloned.1.call-update) | async-done | bytes 2704
  978.5 19.2 %all-reduce.1 = (bf16[5,96]{1,0:T(8,128)(2,1)S(1)}, bf16[5,96]{1,0:T(8,128)(2,1)S(1)}, bf16[5,96]{1,0:T(8,128)(2,1)S(1)}, bf16[7,96]{1,0:T(8,128)(2,1)S(1)}, bf16[7,96]{1,0:T(8,128)(2,1)S(1)}) all-reduce(bf16[5,96]{1,0:T(8,128)(2,1)S(1)} %copy.258, bf16[5,96]{1,0:T(8,128)(2,1)S(1)} %copy.260, ...), channel_id=1, replica_groups=mesh['dp'=4,'fsdp'=8] {'dp'}, use_global_device_ids=true, to_apply=%region_49.50 | all-reduce | flops 2784 | bytes 11136 | tf_op jit(solution)/shard_map/psum | solution.py:373
  1000.7 135.1 %all-reduce.6.cloned.1.call-done = (bf16[4,96,768]{2,0,1:T(4,128)(2,1)}, bf16[4,96,768]{2,1,0:T(8,128)(2,1)}, bf16[4,96,768]{2,1,0:T(8,128)(2,1)}, bf16[2,96,3072]{2,1,0:T(8,128)(2,1)}, bf16[2,96,3072]{2,1,0:T(8,128)(2,1)}) async-done(((bf16[4,96,768]{2,0,1:T(4,128)(2,1)}, bf16[4,96,768]{2,1,0:T(8,128)(2,1)}, bf16[4,96,768]{2,1,0:T(8,128)(2,1)}, bf16[2,96,3072]{2,1,0:T(8,128)(2,1)}, ...) | async-done | bytes 4128784 | tf_op jit(solution)/shard_map/psum | solution.py:372
  (697 shorter events, 351.6 us)
Async XLA Ops:
  7.2 54.4 %all-gather.11.cloned.1.call-start = ((), (), s32[]{:S(2)}) async-start(), calls=%async_computation.9 | async-start | bytes 5308416 | tf_op jit(solution)/shard_map/all_gather | solution.py:190
  7.9 84.7 %all-gather.17.cloned.1.call-start = ((), (), s32[]{:S(2)}) async-start(), calls=%async_computation.12 | async-start | bytes 5308416 | tf_op jit(solution)/shard_map/all_gather | solution.py:209
  8.7 144.7 %all-gather.19.cloned.1.call-start = ((), (), s32[]{:S(2)}) async-start(), calls=%async_computation.13 | async-start | bytes 10616832 | tf_op jit(solution)/shard_map/all_gather | solution.py:229
  9.4 227.9 %all-gather.13.cloned.1.call-start = ((), (), s32[]{:S(2)}) async-start(), calls=%async_computation.10 | async-start | bytes 5308416 | tf_op jit(solution)/shard_map/all_gather | solution.py:207
  10.1 250.3 %all-gather.15.cloned.1.call-start = ((), (), s32[]{:S(2)}) async-start(), calls=%async_computation.11 | async-start | bytes 10616832 | tf_op jit(solution)/shard_map/all_gather | solution.py:227
  10.7 751.2 %reduce-scatter.22.cloned.1.call-start = ((), (), s32[]{:S(2)}) async-start(), calls=%async_computation.15 | async-start | bytes 10616832 | tf_op jit(solution)/shard_map/reduce_scatter | solution.py:325
  228.5 535.5 %reduce-scatter.20.cloned.1.call-start = ((), (), s32[]{:S(2)}) async-start(), calls=%async_computation.14 | async-start | bytes 10616832 | tf_op jit(solution)/shard_map/reduce_scatter | solution.py:323
  312.6 453.9 %reduce-scatter.26.cloned.1.call-start = ((), (), s32[]{:S(2)}) async-start(), calls=%async_computation.17 | async-start | bytes 21233664 | tf_op jit(solution)/shard_map/reduce_scatter | solution.py:277
  327.4 466.1 %reduce-scatter.24.cloned.1.call-start = ((), (), s32[]{:S(2)}) async-start(), calls=%async_computation.16 | async-start | bytes 21233664 | tf_op jit(solution)/shard_map/reduce_scatter | solution.py:275
  340.1 490.1 %reduce-scatter.32.cloned.1.call-start = ((), (), s32[]{:S(2)}) async-start(), calls=%async_computation.20 | async-start | bytes 442368
  446.0 309.8 %copy-start.161 = (f32[12,64]{1,0:T(8,128)S(1)}, f32[12,64]{1,0:T(8,128)}, u32[]{:S(2)}) copy-start(f32[12,64]{1,0:T(8,128)} %get-tuple-element.187) | copy-start | bytes 9220
  446.0 309.9 %copy-start.133 = (f32[768]{0:T(1024)S(1)}, f32[768]{0:T(1024)}, u32[]{:S(2)}) copy-start(f32[768]{0:T(1024)} %get-tuple-element.125) | copy-start | bytes 9220
  446.0 310.1 %copy-start.134 = (f32[768]{0:T(1024)S(1)}, f32[768]{0:T(1024)}, u32[]{:S(2)}) copy-start(f32[768]{0:T(1024)} %get-tuple-element.127) | copy-start | bytes 9220
  446.0 310.1 %copy-start.126 = (f32[768]{0:T(1024)S(1)}, f32[768]{0:T(1024)}, u32[]{:S(2)}) copy-start(f32[768]{0:T(1024)} %get-tuple-element.74) | copy-start | bytes 9220
  446.0 310.0 %copy-start.138 = (f32[768]{0:T(1024)S(1)}, f32[768]{0:T(1024)}, u32[]{:S(2)}) copy-start(f32[768]{0:T(1024)} %get-tuple-element.80) | copy-start | bytes 9220
  446.0 310.1 %copy-start.137 = (f32[768]{0:T(1024)S(1)}, f32[768]{0:T(1024)}, u32[]{:S(2)}) copy-start(f32[768]{0:T(1024)} %get-tuple-element.85) | copy-start | bytes 9220
  446.0 311.2 %copy-start.145 = (f32[3072]{0:T(1024)S(1)}, f32[3072]{0:T(1024)}, u32[]{:S(2)}) copy-start(f32[3072]{0:T(1024)} %get-tuple-element.199) | copy-start | bytes 36868
  446.0 311.2 %copy-start.128 = (f32[768]{0:T(1024)S(1)}, f32[768]{0:T(1024)}, u32[]{:S(2)}) copy-start(f32[768]{0:T(1024)} %get-tuple-element.117) | copy-start | bytes 9220
  446.0 311.2 %copy-start.127 = (f32[768]{0:T(1024)S(1)}, f32[768]{0:T(1024)}, u32[]{:S(2)}) copy-start(f32[768]{0:T(1024)} %get-tuple-element.70) | copy-start | bytes 9220
  446.0 421.1 %reduce-scatter.30.cloned.1.call-start = ((), (), s32[]{:S(2)}) async-start(), calls=%async_computation.19 | async-start | bytes 442368
  756.1 147.8 %reduce-scatter.28.cloned.1.call-start = ((), (), s32[]{:S(2)}) async-start(), calls=%async_computation.18 | async-start | bytes 442368
  757.3 183.6 %reduce-scatter.36.cloned.1.call-start = ((), (), s32[]{:S(2)}) async-start(), calls=%async_computation.22 | async-start | bytes 442368
  758.4 219.3 %reduce-scatter.34.cloned.1.call-start = ((), (), s32[]{:S(2)}) async-start(), calls=%async_computation.21 | async-start | bytes 442368
  759.4 376.4 %all-reduce.6.cloned.1.call-start = ((), (), s32[]{:S(2)}) async-start(), calls=%async_computation.23 | async-start | bytes 8257536 | tf_op jit(solution)/shard_map/psum | solution.py:372
  (182 other events, 2830.1 us)
Sparse Core Ops, SparseCore 0:
  9.9 41.7 all-gather.10
  53.6 38.9 all-gather.16
  94.5 58.8 all-gather.18
  155.1 38.9 all-gather.12
  195.8 58.8 all-gather.14
  258.1 76.4 reduce-scatter.21
  338.1 76.4 reduce-scatter.19
  418.3 201.1 reduce-scatter.25
  623.1 170.3 reduce-scatter.23
  796.4 33.8 reduce-scatter.31
  833.3 33.8 reduce-scatter.29
  870.1 33.8 reduce-scatter.27
  907.0 33.8 reduce-scatter.35
  943.8 33.8 reduce-scatter.33
  981.4 154.3 all-reduce.5
where the time goes:
time: 1160 us; the launch traced here: 1150 us
  blocking collectives  372 us (32%)
  waiting for transfers between devices  341 us (29%)
  matrix products  198 us (17%)
  local copies, waits for them, and re-layouts  147 us (13%)
  other arithmetic  74.4 us (6%)
  between operations  17.7 us (2%)
    unnamed x1, blocking collectives  308 us
    unnamed x20, waiting for transfers between devices  166 us
    psum x1, waiting for transfers between devices, local(): lax.psum(cross_shards[0].astype(jnp.bfloat16), 'dp').astype(jnp.float32)  135 us
    dot_general x20, matrix products, product(): return jnp.dot(left, right, preferred_element_type=jnp.float32)  75.8 us
    dot_general x20, matrix products, through(): lax.dot_general(grad_rows, weight, (((1,), (1,)), ((), ())), preferred_el...  46.5 us
    reshape x16, local copies, waits for them, and re-layouts, split_heads(): return rows.reshape(items, -1, HEADS, rows.shape[-1] // HEADS)  39.1 us
    unnamed x394, local copies, waits for them, and re-layouts  35.2 us
    dot_general x20, matrix products, outer(): lax.dot_general(left, right, (((0,), (0,)), ((), ())), preferred_element_...  26.4 us
  transfers between devices with their start and end apart: 15, of which 9 were waited for; matrix products, arithmetic and copies ran while one was open for 34% of the time, Pallas kernels for 0%

commit v1 on v0

v1 whole, which is shorter than its diff:
```python
from functools import partial

import jax
import jax.numpy as jnp
from jax import lax
from jax.sharding import PartitionSpec as P
from jax.experimental import pallas as pl
from jax.experimental.pallas import tpu as pltpu

HEADS = 12
epsilon = 1e-12
negative = -10000.0
bf16 = jnp.bfloat16
f32 = jnp.float32

CROSS, WORD_SELF, REGION_SELF, WORD_FEED, REGION_FEED = 0, 5, 10, 15, 22
VECTOR_ROWS = 32


def nn(left, right):
    return jnp.dot(left, right, preferred_element_type=f32)


def nt(left, right):
    return lax.dot_general(left, right, (((1,), (1,)), ((), ())), preferred_element_type=f32)


def tn(left, right):
    return lax.dot_general(left, right, (((0,), (0,)), ((), ())), preferred_element_type=f32)


def norm_parts(total):
    centred = total - jnp.mean(total, axis=-1, keepdims=True)
    spread = jnp.mean(centred * centred, axis=-1, keepdims=True)
    rate = lax.rsqrt(spread + epsilon)
    return centred * rate, rate


def norm_back(grad, unit, rate, gain):
    scaled = grad * gain
    mean_one = jnp.mean(scaled, axis=-1, keepdims=True)
    mean_two = jnp.mean(scaled * unit, axis=-1, keepdims=True)
    return (
        rate * (scaled - mean_one - unit * mean_two),
        jnp.sum(grad * unit, axis=0, keepdims=True),
        jnp.sum(grad, axis=0, keepdims=True),
    )


def half_masks(rows):
    lane = lax.broadcasted_iota(jnp.int32, (rows, 128), 1)
    return (lane < 64, lane >= 64)


def heads_forward(q_ref, k_ref, v_ref, bias_ref, probs_ref, ctx_ref):
    blocks, qb, kb = bias_ref.shape
    pairs = q_ref.shape[1] // 128
    masks = half_masks(kb)
    zero = jnp.zeros((kb, 128), bf16)

    def block(b, carry):
        rq = pl.ds(pl.multiple_of(b * qb, 16), qb)
        rk = pl.ds(pl.multiple_of(b * kb, 16), kb)
        bias = bias_ref[b]
        for p in range(pairs):
            cols = pl.ds(p * 128, 128)
            qp = q_ref[rq, cols]
            kp = k_ref[rk, cols]
            vp = v_ref[rk, cols]
            mixed = None
            for half in range(2):
                s = nt(qp, jnp.where(masks[half], kp, zero)) * 0.125 + bias
                e = jnp.exp(s - jnp.max(s, axis=-1, keepdims=True))
                low = (e / jnp.sum(e, axis=-1, keepdims=True)).astype(bf16)
                probs_ref[b * (2 * pairs) + 2 * p + half] = low
                part = nn(low, jnp.where(masks[half], vp, zero))
                mixed = part if mixed is None else mixed + part
            ctx_ref[rq, cols] = mixed.astype(bf16)
        return carry

    lax.fori_loop(0, blocks, block, 0)


def heads_backward(q_ref, k_ref, v_ref, probs_ref, dctx_ref, dq_ref, dk_ref, dv_ref, blocks):
    qb = q_ref.shape[0] // blocks
    kb = k_ref.shape[0] // blocks
    pairs = q_ref.shape[1] // 128
    kmasks, qmasks = half_masks(kb), half_masks(qb)
    kzero, qzero = jnp.zeros((kb, 128), bf16), jnp.zeros((qb, 128), bf16)

    def block(b, carry):
        rq = pl.ds(pl.multiple_of(b * qb, 16), qb)
        rk = pl.ds(pl.multiple_of(b * kb, 16), kb)
        for p in range(pairs):
            cols = pl.ds(p * 128, 128)
            qp = q_ref[rq, cols]
            kp = k_ref[rk, cols]
            vp = v_ref[rk, cols]
            dc = dctx_ref[rq, cols]
            dq = dk = dv = 0.0
            for half in range(2):
                low = probs_ref[b * (2 * pairs) + 2 * p + half]
                probs = low.astype(f32)
                dp = nt(dc, jnp.where(kmasks[half], vp, kzero))
                dv = dv + tn(low, jnp.where(qmasks[half], dc, qzero))
                t = probs * dp
                ds = (t - probs * jnp.sum(t, axis=-1, keepdims=True)).astype(bf16)
                dq = dq + nn(ds, jnp.where(kmasks[half], kp, kzero))
                dk = dk + tn(ds, jnp.where(qmasks[half], qp, qzero))
            dq_ref[rq, cols] = (dq * 0.125).astype(bf16)
            dk_ref[rk, cols] = (dk * 0.125).astype(bf16)
            dv_ref[rk, cols] = dv.astype(bf16)
        return carry

    lax.fori_loop(0, blocks, block, 0)


def vec(vec_ref, row):
    return vec_ref[row : row + 1, :]


def attend(x_low, c_low, base, w_ref, vec_ref, row, bias_ref, q_ref, k_ref, v_ref, probs_ref, ctx_ref):
    q_ref[...] = (nn(x_low, w_ref[0]) + vec(vec_ref, row)).astype(bf16)
    k_ref[...] = nn(c_low, w_ref[1]).astype(bf16)
    v_ref[...] = (nn(c_low, w_ref[2]) + vec(vec_ref, row + 1)).astype(bf16)
    heads_forward(q_ref, k_ref, v_ref, bias_ref, probs_ref, ctx_ref)
    return base + nn(ctx_ref[...], w_ref[3]) + vec(vec_ref, row + 2)


def cross_forward_kernel(
    words_ref, regions_ref, w_ref, vec_ref, wr_ref, rw_ref,
    wtot_ref, rtot_ref, wq_ref, wk_ref, wv_ref, wp_ref, wc_ref, rq_ref, rk_ref, rv_ref, rp_ref, rc_ref,
):
    words, regions = words_ref[...], regions_ref[...]
    wtot_ref[...] = attend(words, regions, words.astype(f32), w_ref, vec_ref, CROSS, wr_ref, wq_ref, wk_ref, wv_ref, wp_ref, wc_ref)
    rtot_ref[...] = attend(regions, words, regions.astype(f32), w_ref, vec_ref, CROSS, rw_ref, rq_ref, rk_ref, rv_ref, rp_ref, rc_ref)


def self_forward_kernel(row, tot_ref, w_ref, vec_ref, bias_ref, out_ref, q_ref, k_ref, v_ref, p_ref, c_ref):
    unit, _ = norm_parts(tot_ref[...])
    y = unit * vec(vec_ref, CROSS + 3) + vec(vec_ref, CROSS + 4)
    low = y.astype(bf16)
    out_ref[...] = attend(low, low, y, w_ref, vec_ref, row, bias_ref, q_ref, k_ref, v_ref, p_ref, c_ref)


def gelu_parts(x):
    size = jnp.abs(x)
    e = jnp.exp(x * x * -0.5)
    t = 1.0 / (1.0 + (0.3275911 * 0.7071067811865476) * size)
    poly = t * (0.127414796 + t * (-0.142248368 + t * (0.7107068705 + t * (-0.7265760135 + t * 0.5307027145))))
    tail = poly * e
    phi = jnp.where(x >= 0, 1.0 - tail, tail)
    return x * phi, phi + x * e * 0.3989422804014327


def slot_of(s, me, order):
    k = s ^ me
    slot = 0
    for bit in order:
        slot = slot * 2 + ((k >> bit) & 1)
    return slot


def place(dest_ref, value, me, order):
    if order is None:
        dest_ref[...] = value
        return
    rows = value.shape[0] // SLOTS
    for s in range(SLOTS):
        slot = slot_of(s, me, order)
        dest_ref[pl.ds(pl.multiple_of(slot * rows, 16), rows), :] = value[s * rows : (s + 1) * rows, :]


SLOTS = 8


def put(keep_ref, send_ref, base, stride, cols, value):
    rows = value.shape[0] // SLOTS
    low = value.astype(bf16)
    for j in range(SLOTS):
        dest = keep_ref if j < SLOTS // 2 else send_ref
        start = base + (j % (SLOTS // 2)) * stride
        dest[start : start + rows, cols] = low[j * rows : (j + 1) * rows]


def feed_kernel(
    self_row, row, chunk, orders,
    me_ref, tot_ref, cot_ref, m_ref, vec_ref,
    out_ref, dtot_ref, keep_ref, send_ref, dvec_ref,
    x_ref, y_ref, h_ref, gp_ref, dpre_ref, dy_ref, xt_ref, dyt_ref, acc_ref, bup_ref, dbup_ref,
):
    me = me_ref[0]
    width = tot_ref.shape[1]
    hidden = m_ref.shape[2]
    parts = hidden // width
    block = width // SLOTS
    for i in range(parts):
        bup_ref[:, i * width : (i + 1) * width] = vec(vec_ref, row + i)
    unit2, rate2 = norm_parts(tot_ref[...])
    y = unit2 * vec(vec_ref, self_row + 3) + vec(vec_ref, self_row + 4)
    y_ref[...] = y
    x_ref[...] = y.astype(bf16)

    def up(i, carry):
        cols = pl.ds(pl.multiple_of(i * chunk, 128), chunk)
        pre = nn(x_ref[...], m_ref[0, :, cols]) + bup_ref[:, cols]
        value, slope = gelu_parts(pre)
        h_ref[:, cols] = value.astype(bf16)
        gp_ref[:, cols] = slope
        return carry

    lax.fori_loop(0, hidden // chunk, up, 0)

    def down(i, carry):
        cols = pl.ds(pl.multiple_of(i * 256, 128), 256)
        acc_ref[:, cols] = nt(h_ref[...], m_ref[1, pl.ds(pl.multiple_of(i * 256, 16), 256), :])
        return carry

    lax.fori_loop(0, width // 256, down, 0)
    gain = vec(vec_ref, row + 5)
    unit, rate = norm_parts(y_ref[...] + acc_ref[...] + vec(vec_ref, row + 4))
    out_ref[...] = (unit * gain + vec(vec_ref, row + 6)).astype(bf16)
    dtot, dgain, dshift = norm_back(cot_ref[...].astype(f32), unit, rate, gain)
    dy = dtot.astype(bf16)
    dy_ref[...] = dy
    dvec_ref[...] = jnp.zeros_like(dvec_ref)
    dvec_ref[row + 4 : row + 5, :] = jnp.sum(dy.astype(f32), axis=0, keepdims=True)
    dvec_ref[row + 5 : row + 6, :] = dgain
    dvec_ref[row + 6 : row + 7, :] = dshift
    y_ref[...] = dtot
    place(xt_ref, x_ref[...].T, me, orders[0])
    place(dyt_ref, dy.T, me, orders[1])

    def back(i, carry):
        cols = pl.ds(pl.multiple_of(i * chunk, 128), chunk)
        dpre = (nn(dy_ref[...], m_ref[1, :, cols]) * gp_ref[:, cols]).astype(bf16)
        dpre_ref[:, cols] = dpre
        dbup_ref[:, cols] = jnp.sum(dpre.astype(f32), axis=0, keepdims=True)
        put(keep_ref, send_ref, 0, block, cols, nn(xt_ref[...], dpre))
        put(keep_ref, send_ref, width // 2, block, cols, nn(dyt_ref[...], h_ref[:, cols]))
        return carry

    lax.fori_loop(0, hidden // chunk, back, 0)
    for i in range(parts):
        dvec_ref[row + i : row + i + 1, :] = dbup_ref[:, i * width : (i + 1) * width]

    def rows(i, carry):
        cols = pl.ds(pl.multiple_of(i * 256, 128), 256)
        acc_ref[:, cols] = nt(dpre_ref[...], m_ref[0, pl.ds(pl.multiple_of(i * 256, 16), 256), :])
        return carry

    lax.fori_loop(0, width // 256, rows, 0)
    unit2, rate2 = norm_parts(tot_ref[...])
    dtot2, dgain2, dshift2 = norm_back(acc_ref[...] + y_ref[...], unit2, rate2, vec(vec_ref, self_row + 3))
    dtot_ref[...] = dtot2
    dvec_ref[self_row + 3 : self_row + 4, :] = dgain2
    dvec_ref[self_row + 4 : self_row + 5, :] = dshift2


def column_sum(low):
    return jnp.sum(low.astype(f32), axis=0, keepdims=True)


def self_backward_kernel(
    row, blocks, orders,
    me_ref, dtot_ref, tot_ref, w_ref, vec_ref, q_ref, k_ref, v_ref, p_ref, c_ref,
    out_ref, keep_ref, send_ref, dvec_ref,
    dq_ref, dk_ref, dv_ref, dc_ref, xp_ref, xq_ref, ct_ref,
):
    me = me_ref[0]
    da = dtot_ref[...].astype(bf16)
    dvec_ref[...] = jnp.zeros_like(dvec_ref)
    dvec_ref[row + 2 : row + 3, :] = column_sum(da)
    dc_ref[...] = nt(da, w_ref[3]).astype(bf16)
    place(ct_ref, c_ref[...].T, me, orders[0])
    width = w_ref.shape[2]
    every = pl.ds(0, width)
    block = width // SLOTS
    put(keep_ref, send_ref, block, 2 * block, every, nn(ct_ref[...], da))
    heads_backward(q_ref, k_ref, v_ref, p_ref, dc_ref, dq_ref, dk_ref, dv_ref, blocks)
    unit, rate = norm_parts(tot_ref[...])
    gain = vec(vec_ref, CROSS + 3)
    low = (unit * gain + vec(vec_ref, CROSS + 4)).astype(bf16)
    turned = low.T
    place(xp_ref, turned, me, orders[0])
    place(xq_ref, turned, me, orders[1])
    dq, dk, dv = dq_ref[...], dk_ref[...], dv_ref[...]
    put(keep_ref, send_ref, 0, 2 * block, every, nn(xp_ref[...], dq))
    put(keep_ref, send_ref, width, 2 * block, every, nn(xq_ref[...], dk))
    put(keep_ref, send_ref, width + block, 2 * block, every, nn(xq_ref[...], dv))
    dvec_ref[row : row + 1, :] = column_sum(dq)
    dvec_ref[row + 1 : row + 2, :] = column_sum(dv)
    dx = dtot_ref[...] + nt(dq, w_ref[0]) + nt(dk, w_ref[1]) + nt(dv, w_ref[2])
    dtot, dgain, dshift = norm_back(dx, unit, rate, gain)
    out_ref[...] = dtot
    dvec_ref[CROSS + 3 : CROSS + 4, :] = dgain
    dvec_ref[CROSS + 4 : CROSS + 5, :] = dshift


def cross_backward_kernel(
    blocks, orders,
    me_ref, dw_ref, dr_ref, words_ref, regions_ref, w_ref, va_ref, vb_ref, vc_ref, vd_ref,
    wq_ref, wk_ref, wv_ref, wp_ref, wc_ref, rq_ref, rk_ref, rv_ref, rp_ref, rc_ref,
    wout_ref, rout_ref, keep_ref, send_ref,
    wdq_ref, wdk_ref, wdv_ref, wdc_ref, rdq_ref, rdk_ref, rdv_ref, rdc_ref, wt_ref, rt_ref, wp2_ref, rp2_ref, wq2_ref, rq2_ref, dvec_ref, vt_ref,
):
    me = me_ref[0]
    width = w_ref.shape[2]
    every = pl.ds(0, width)
    block = width // SLOTS
    stride = 2 * block + VECTOR_ROWS
    second = stride * (SLOTS // 2)
    wda, rda = dw_ref[...].astype(bf16), dr_ref[...].astype(bf16)
    dvec_ref[...] = va_ref[...] + vb_ref[...] + vc_ref[...] + vd_ref[...]
    dvec_ref[CROSS + 2 : CROSS + 3, :] = column_sum(wda) + column_sum(rda)
    wdc_ref[...] = nt(wda, w_ref[3]).astype(bf16)
    rdc_ref[...] = nt(rda, w_ref[3]).astype(bf16)
    heads_backward(wq_ref, wk_ref, wv_ref, wp_ref, wdc_ref, wdq_ref, wdk_ref, wdv_ref, blocks)
    heads_backward(rq_ref, rk_ref, rv_ref, rp_ref, rdc_ref, rdq_ref, rdk_ref, rdv_ref, blocks)
    place(wt_ref, wc_ref[...].T, me, orders[0])
    place(rt_ref, rc_ref[...].T, me, orders[0])
    put(keep_ref, send_ref, block, stride, every, nn(wt_ref[...], wda) + nn(rt_ref[...], rda))
    words_t, regions_t = words_ref[...].T, regions_ref[...].T
    place(wp2_ref, words_t, me, orders[0])
    place(rp2_ref, regions_t, me, orders[0])
    wdq, wdk, wdv = wdq_ref[...], wdk_ref[...], wdv_ref[...]
    rdq, rdk, rdv = rdq_ref[...], rdk_ref[...], rdv_ref[...]
    put(keep_ref, send_ref, 0, stride, every, nn(wp2_ref[...], wdq) + nn(rp2_ref[...], rdq))
    place(wq2_ref, words_t, me, orders[1])
    place(rq2_ref, regions_t, me, orders[1])
    put(keep_ref, send_ref, second, 2 * block, every, nn(rq2_ref[...], wdk) + nn(wq2_ref[...], rdk))
    put(keep_ref, send_ref, second + block, 2 * block, every, nn(rq2_ref[...], wdv) + nn(wq2_ref[...], rdv))
    dvec_ref[CROSS : CROSS + 1, :] = column_sum(wdq) + column_sum(rdq)
    dvec_ref[CROSS + 1 : CROSS + 2, :] = column_sum(wdv) + column_sum(rdv)
    vt_ref[...] = jnp.zeros_like(vt_ref)
    for s in range(SLOTS):
        slot = s if orders[0] is None else slot_of(s, me, orders[0])
        vt_ref[pl.ds(pl.multiple_of(slot * VECTOR_ROWS, 16), VECTOR_ROWS), 0:block] = dvec_ref[:, s * block : (s + 1) * block].astype(bf16)
    for j in range(SLOTS):
        dest = keep_ref if j < SLOTS // 2 else send_ref
        start = (j % (SLOTS // 2)) * stride + 2 * block
        dest[start : start + VECTOR_ROWS, :] = vt_ref[j * VECTOR_ROWS : (j + 1) * VECTOR_ROWS, :]
    wout_ref[...] = (dw_ref[...] + nt(wdq, w_ref[0]) + nt(rdk, w_ref[1]) + nt(rdv, w_ref[2])).astype(bf16)
    rout_ref[...] = (dr_ref[...] + nt(rdq, w_ref[0]) + nt(wdk, w_ref[1]) + nt(wdv, w_ref[2])).astype(bf16)


VMEM_LIMIT = 60 * 1024 * 1024


def call(kernel, name, outs, scratch, flops, args, scalar=False):
    whole = pl.BlockSpec(memory_space=pltpu.VMEM)
    specs = [whole] * len(args)
    if scalar:
        specs[0] = pl.BlockSpec(memory_space=pltpu.SMEM)
    out_shape = tuple(jax.ShapeDtypeStruct(s, d) for s, d in outs)
    moved = sum(a.size * a.dtype.itemsize for a in args) + sum(o.size * o.dtype.itemsize for o in out_shape)
    return pl.pallas_call(
        kernel,
        out_shape=out_shape,
        in_specs=specs,
        out_specs=tuple([whole] * len(outs)),
        scratch_shapes=[pltpu.VMEM(s, d) for s, d in scratch],
        compiler_params=pltpu.CompilerParams(vmem_limit_bytes=VMEM_LIMIT),
        cost_estimate=pl.CostEstimate(flops=int(flops), bytes_accessed=int(moved), transcendentals=0),
        name=name,
    )(*args)


def kept_shapes(nq, nk, width, bias):
    blocks, qb, kb = bias.shape
    return [((nq, width), bf16), ((nk, width), bf16), ((nk, width), bf16), ((blocks * HEADS, qb, kb), bf16), ((nq, width), bf16)]


def cross_forward(words, regions, w, vectors, wr, rw):
    nw, nr, width = words.shape[0], regions.shape[0], words.shape[1]
    outs = [((nw, width), f32), ((nr, width), f32)] + kept_shapes(nw, nr, width, wr) + kept_shapes(nr, nw, width, rw)
    got = call(cross_forward_kernel, "cross_forward", outs, [], 8.0 * (nw + nr) * width * width, (words, regions, w, vectors, wr, rw))
    return got[0], got[1], got[2:7], got[7:12]


def self_forward(row, total, w, vectors, bias):
    n, width = total.shape
    outs = [((n, width), f32)] + kept_shapes(n, n, width, bias)
    got = call(partial(self_forward_kernel, row), "self_forward", outs, [], 8.0 * n * width * width, (total, w, vectors, bias))
    return got[0], got[1:]


def feed_both(self_row, row, orders, me, total, cot, m, vectors):
    n, width = total.shape
    hidden = m.shape[2]
    half = (width, hidden)
    outs = [((n, width), bf16), ((n, width), f32), (half, bf16), (half, bf16), ((VECTOR_ROWS, width), f32)]
    scratch = [
        ((n, width), bf16), ((n, width), f32), ((n, hidden), bf16), ((n, hidden), f32), ((n, hidden), bf16),
        ((n, width), bf16), ((width, n), bf16), ((width, n), bf16), ((n, width), f32), ((1, hidden), f32), ((1, hidden), f32),
    ]
    return call(partial(feed_kernel, self_row, row, 512, orders), "feed", outs, scratch, 12.0 * n * width * hidden, (me, total, cot, m, vectors), scalar=True)


def self_backward(row, blocks, orders, me, dtot, total, w, vectors, kept):
    n, width = total.shape
    half = (2 * width, width)
    outs = [((n, width), f32), (half, bf16), (half, bf16), ((VECTOR_ROWS, width), f32)]
    scratch = [((n, width), bf16)] * 4 + [((width, n), bf16)] * 3
    return call(partial(self_backward_kernel, row, blocks, orders), "self_backward", outs, scratch, 16.0 * n * width * width, (me, dtot, total, w, vectors, *kept), scalar=True)


def cross_backward(blocks, orders, me, dw, dr, words, regions, w, dvecs, word_kept, region_kept):
    nw, nr, width = words.shape[0], regions.shape[0], words.shape[1]
    half = (2 * width + VECTOR_ROWS * (SLOTS // 2), width)
    outs = [((nw, width), bf16), ((nr, width), bf16), (half, bf16), (half, bf16)]
    scratch = [((nw, width), bf16), ((nr, width), bf16), ((nr, width), bf16), ((nw, width), bf16)]
    scratch += [((nr, width), bf16), ((nw, width), bf16), ((nw, width), bf16), ((nr, width), bf16)]
    scratch += [((width, nw), bf16), ((width, nr), bf16)] * 3
    scratch += [((VECTOR_ROWS, width), f32), ((VECTOR_ROWS * SLOTS, width), bf16)]
    return call(partial(cross_backward_kernel, blocks, orders), "cross_backward", outs, scratch, 16.0 * (nw + nr) * width * width, (me, dw, dr, words, regions, w, *dvecs, *word_kept, *region_kept), scalar=True)


def block_bias(query_slots, key_slots, key_bias, blocks):
    items = key_bias.shape[0] // blocks
    rows = jnp.arange(items * query_slots) // query_slots
    cols = jnp.arange(items * key_slots) // key_slots
    same = rows[:, None] == cols[None, :]
    return jnp.where(same[None], key_bias.reshape(blocks, 1, items * key_slots), -1e30).astype(f32)


def reduce_pieces(keep, send, first):
    def exchange(value, bit):
        return lax.ppermute(value, "fsdp", [(i, i ^ (1 << bit)) for i in range(SLOTS)])

    def add(left, right):
        return (left.astype(f32) + right.astype(f32)).astype(bf16)

    got = exchange(send, 0)
    cut = first
    rest = keep.shape[0]
    done = []
    for (low, high), bits in zip(((0, cut), (cut, rest)), ((1, 2), (2, 1))):
        half = (high - low) // 2
        mid = low + half
        sent = add(keep[mid:high], got[mid:high])
        held = add(keep[low:mid], got[low:mid])
        back = exchange(sent, bits[0])
        quarter = half // 2
        sent = add(held[quarter:], back[quarter:])
        held = add(held[:quarter], back[:quarter])
        back = exchange(sent, bits[1])
        done.append(add(held, back))
    return done


def local(
    words_in, regions_in, word_mask, region_count,
    cross_matrices, cross_vectors, word_self_matrices, word_self_vectors,
    region_self_matrices, region_self_vectors, word_feed_matrices, word_feed_vectors,
    region_feed_matrices, region_feed_vectors, words_cotangent, regions_cotangent,
):
    items, words, width = words_in.shape
    regions = regions_in.shape[1]
    share = cross_matrices.shape[1]
    count = width // share
    blocks = 3 if items % 12 == 0 else 1
    swaps = count == SLOTS
    orders = ((0, 1, 2), (0, 2, 1)) if swaps else (None, None)
    me = lax.axis_index("fsdp").astype(jnp.int32).reshape(1)

    own = jnp.concatenate([cross_vectors, word_self_vectors, region_self_vectors, word_feed_vectors, region_feed_vectors], axis=0)
    own = jnp.pad(own, ((0, VECTOR_ROWS - own.shape[0]), (0, 0)))
    vectors = lax.all_gather(own, "fsdp", axis=1, tiled=True).astype(f32)

    def whole(shard):
        return lax.all_gather(shard, "fsdp", axis=1, tiled=True)

    cross = whole(cross_matrices)
    region_self = whole(region_self_matrices)
    word_self = whole(word_self_matrices)
    region_feed = whole(region_feed_matrices)
    word_feed = whole(word_feed_matrices)

    word_bias = (word_mask.astype(f32) - 1.0) * 10000.0
    region_bias = jnp.where(jnp.arange(regions)[None, :] < region_count[:, None], 0.0, negative).astype(f32)
    word_rows = words_in.reshape(-1, width)
    region_rows = regions_in.reshape(-1, width)
    wr = block_bias(words, regions, region_bias, blocks)
    rw = block_bias(regions, words, word_bias, blocks)
    ww = block_bias(words, words, word_bias, blocks)
    rr = block_bias(regions, regions, region_bias, blocks)

    word_one, region_one, word_kept, region_kept = cross_forward(word_rows, region_rows, cross, vectors, wr, rw)
    region_two, region_self_kept = self_forward(REGION_SELF, region_one, region_self, vectors, rr)
    word_two, word_self_kept = self_forward(WORD_SELF, word_one, word_self, vectors, ww)
    regions_out, region_dtwo, region_feed_keep, region_feed_send, dvec_a = feed_both(
        REGION_SELF, REGION_FEED, orders, me, region_two, regions_cotangent.reshape(-1, width), region_feed, vectors
    )
    region_done, region_self_keep, region_self_send, dvec_b = self_backward(
        REGION_SELF, blocks, orders, me, region_dtwo, region_one, region_self, vectors, region_self_kept
    )
    words_out, word_dtwo, word_feed_keep, word_feed_send, dvec_c = feed_both(
        WORD_SELF, WORD_FEED, orders, me, word_two, words_cotangent.reshape(-1, width), word_feed, vectors
    )
    word_done, word_self_keep, word_self_send, dvec_d = self_backward(
        WORD_SELF, blocks, orders, me, word_dtwo, word_one, word_self, vectors, word_self_kept
    )
    words_grad, regions_grad, cross_keep, cross_send = cross_backward(
        blocks, orders, me, word_done, region_done, word_rows, region_rows, cross,
        (dvec_a, dvec_b, dvec_c, dvec_d), word_kept, region_kept,
    )

    half = SLOTS // 2
    block = width // SLOTS
    names = ["region_feed", "region_self", "word_feed", "word_self", "cross"]
    pairs = [
        (region_feed_keep, region_feed_send), (region_self_keep, region_self_send), (word_feed_keep, word_feed_send),
        (word_self_keep, word_self_send), (cross_keep, cross_send),
    ]
    grads = {}
    for name, (keep, send) in zip(names, pairs):
        per = [block, block] if "feed" in name else [2 * block, 2 * block]
        if name == "cross":
            per[0] += VECTOR_ROWS
        if swaps:
            first, second = reduce_pieces(keep, send, half * per[0])
        else:
            whole_rows = jnp.concatenate([keep[: half * per[0]], send[: half * per[0]], keep[half * per[0] :], send[half * per[0] :]])
            cut = SLOTS * per[0]
            first = whole_rows[:cut].reshape(SLOTS, per[0], -1)
            second = whole_rows[cut:].reshape(SLOTS, per[1], -1)

            def scattered(rows):
                joined = rows.reshape(SLOTS, -1, block, rows.shape[-1]).transpose(1, 0, 2, 3)
                joined = joined.reshape(-1, width, rows.shape[-1])
                return lax.psum_scatter(joined, "fsdp", scatter_dimension=1, tiled=True).reshape(-1, rows.shape[-1])

            if name == "cross":
                tail = first[:, 2 * block :, :block].transpose(1, 0, 2).reshape(VECTOR_ROWS, width)
                vector_shard = lax.psum_scatter(tail, "fsdp", scatter_dimension=1, tiled=True)
                first = first[:, : 2 * block]
            first, second = scattered(first), scattered(second)
        grads[name] = (first, second)
    result = {}
    for name in names:
        first, second = grads[name]
        if name == "cross" and swaps:
            first, second, vector_shard = lax.psum((first[: 2 * share], second, first[2 * share :, :share]), "dp")
            vector_sum = vector_shard
        elif name == "cross":
            first, second, vector_sum = lax.psum((first, second, vector_shard), "dp")
        else:
            first, second = lax.psum((first, second), "dp")
        if "feed" in name:
            result[name] = jnp.stack([first, second]).astype(f32)
        else:
            result[name] = jnp.stack([first[:share], second[:share], second[share:], first[share:]]).astype(f32)
    vector_sum = vector_sum.astype(f32)

    def rows_of(start, number):
        return vector_sum[start : start + number]

    return (
        words_out.reshape(items, words, width),
        regions_out.reshape(items, regions, width),
        words_grad.reshape(items, words, width),
        regions_grad.reshape(items, regions, width),
        result["cross"],
        rows_of(CROSS, 5),
        result["word_self"],
        rows_of(WORD_SELF, 5),
        result["region_self"],
        rows_of(REGION_SELF, 5),
        result["word_feed"],
        rows_of(WORD_FEED, 7),
        result["region_feed"],
        rows_of(REGION_FEED, 7),
    )


def solution(mesh):
    items = P(("dp", "fsdp"), None, None)
    matrix = P(None, "fsdp", None)
    vector = P(None, "fsdp")
    weights = (matrix, vector) * 5
    return jax.shard_map(
        local,
        mesh=mesh,
        in_specs=(items, items, P(("dp", "fsdp"), None), P(("dp", "fsdp")), *weights, items, items),
        out_specs=(items,) * 4 + weights,
        check_vma=False,
    )
```

time: 1160 us -> 645 us (0.56)
  blocking collectives: 372 us -> 23.5 us
  matrix products: 198 us -> 0 us
  Pallas kernels: 0 us -> 152 us
  local copies, waits for them, and re-layouts: 147 us -> 14.7 us
  other arithmetic: 74.4 us -> 27.7 us
  waiting for transfers between devices: 341 us -> 386 us
  starting transfers between devices: 1.07 us -> 22.5 us
    unnamed x1 -> x0, blocking collectives: 308 us -> none
    dot_general x84 -> x0, matrix products: 198 us -> none  [the longest x20 75.8 us: product(): return jnp.dot(left, right, preferred_element_type=jnp.float32)]
    unnamed x20 -> x6, waiting for transfers between devices: 166 us -> 3.13 us
    pallas_call x0 -> x8, Pallas kernels: none -> 152 us  [call(): pl.pallas_call(kernel, out_shape=out_shape, in_specs=specs, out_specs=tup...]
    all_gather x5, waiting for transfers between devices: 15.9 us -> 137 us  [whole(): return lax.all_gather(shard, 'fsdp', axis=1, tiled=True)]
    ppermute x0 -> x25, waiting for transfers between devices: none -> 109 us  [exchange(): lax.ppermute(value, 'fsdp', [(i, i ^ 1 << bit) for i in range(SLOTS)])]
    convert_element_type x40 -> x2, local copies, waits for them, and re-layouts: 49.9 us -> 0.76 us  [local(): vectors = lax.all_gather(own, 'fsdp', axis=1, tiled=True).astype(f32)]
    reshape x30 -> x6, local copies, waits for them, and re-layouts: 44 us -> 5.46 us  [the longest x1 0.99 us: local(): regions_cotangent.reshape(-1, width)]
  transfers between devices with their start and end apart: 15 -> 31, of which waited for: 9 -> 19; matrix products, arithmetic and copies ran while one was open for 34% -> 5% of each run, Pallas kernels for 0% -> 24%
where the time goes in v1:
time: 645 us; the launch traced here: 642 us
  waiting for transfers between devices  386 us (60%)
  Pallas kernels  152 us (24%)
  other arithmetic  27.7 us (4%)
  blocking collectives  23.5 us (4%)
  starting transfers between devices  22.5 us (3%)
  local copies, waits for them, and re-layouts  14.7 us (2%)
  between operations  14.7 us (2%)
    pallas_call x8, Pallas kernels, call(): pl.pallas_call(kernel, out_shape=out_shape, in_specs=specs, out_specs=tup...  152 us
    psum x1, waiting for transfers between devices, local(): lax.psum((first[:2 * share], second, first[2 * share:, :share]), 'dp')  137 us
    all_gather x5, waiting for transfers between devices, whole(): return lax.all_gather(shard, 'fsdp', axis=1, tiled=True)  137 us
    ppermute x25, waiting for transfers between devices, exchange(): lax.ppermute(value, 'fsdp', [(i, i ^ 1 << bit) for i in range(SLOTS)])  109 us
    ppermute x25, starting transfers between devices, exchange(): lax.ppermute(value, 'fsdp', [(i, i ^ 1 << bit) for i in range(SLOTS)])  22.3 us
    convert_element_type x22, other arithmetic, add(): return (left.astype(f32) + right.astype(f32)).astype(bf16)  14.5 us
  transfers between devices with their start and end apart: 31, of which 19 were waited for; matrix products, arithmetic and copies ran while one was open for 5% of the time, Pallas kernels for 24%

profile of v1, /device:TPU:0, one launch (start us, length us, event | category | flops | bytes accessed | tf_op | source)
XLA Modules:
  0.0 641.8 jit_solution(12784331060130984773)
XLA Ops:
  11.1 10.7 %all-gather = bf16[8,96,32]{1,2,0:T(8,128)(2,1)S(1)} all-gather(bf16[1,96,32]{1,2,0:T(8,128)(2,1)S(1)} %pad_bitcast_fusion), channel_id=1, replica_groups=mesh['dp'=4,'fsdp'=8] {'fsdp'}, dimensions={0}, use_global_device_ids=true | all-gather | bytes 55296 | tf_op jit(solution)/shard_map/all_gather | solution.py:469
  29.9 21.7 %all-gather.7.cloned.1.call-done.w_ref = bf16[4,768,768]{2,1,0:T(8,128)(2,1)} async-done(((bf16[4,96,768]{2,1,0:T(8,128)(2,1)}), bf16[4,768,768]{2,1,0:T(8,128)(2,1)}) %all-gather.7.cloned.1.call-update) | async-done | bytes 4718608 | tf_op jit(solution)/shard_map/all_gather | solution.py:472
  51.6 18.7 %cross_forward.1 = (f32[240,768]{1,0:T(8,128)}, f32[432,768]{1,0:T(8,128)}, bf16[240,768]{1,0:T(8,128)(2,1)}, bf16[432,768]{1,0:T(8,128)(2,1)}, bf16[432,768]{1,...) custom-call(bf16[240,768]{1,0:T(8,128)(2,1)} %reshape.240.words_ref,, ...), custom_call_target="tpu_custom_call" | custom-call | flops 3170893824 | bytes 13977600 | tf_op jit(solution)/shard_map/cross_forward/pallas_call | solution.py:357
  70.3 22.2 %all-gather.9.cloned.1.call-done.w_ref = bf16[4,768,768]{2,1,0:T(8,128)(2,1)} async-done(((bf16[4,96,768]{2,1,0:T(8,128)(2,1)}), bf16[4,768,768]{2,1,0:T(8,128)(2,1)}) %all-gather.9.cloned.1.call-update) | async-done | bytes 4718608 | tf_op jit(solution)/shard_map/all_gather | solution.py:472
  92.5 7.9 %self_forward.2 = (f32[240,768]{1,0:T(8,128)}, bf16[240,768]{1,0:T(8,128)(2,1)}, bf16[240,768]{1,0:T(8,128)(2,1)}, bf16[240,768]{1,0:T(8,128)(2,1)}, bf16[36,80,...) custom-call(f32[240,768]{1,0:T(8,128)} %get-tuple-element.60.tot_ref, ...), custom_call_target="tpu_custom_call" | custom-call | flops 1132462080 | bytes 8303616 | tf_op jit(solution)/shard_map/self_forward/pallas_call | solution.py:357
  100.3 33.0 %all-gather.13.cloned.1.call-done.w_ref = bf16[4,768,768]{2,1,0:T(8,128)(2,1)} async-done(((bf16[4,96,768]{2,1,0:T(8,128)(2,1)}), bf16[4,768,768]{2,1,0:T(8,128)(2,1)}) %all-gather.13.cloned.1.call-update) | async-done | bytes 4718608 | tf_op jit(solution)/shard_map/all_gather | solution.py:472
  133.3 10.8 %self_forward.3 = (f32[432,768]{1,0:T(8,128)}, bf16[432,768]{1,0:T(8,128)(2,1)}, bf16[432,768]{1,0:T(8,128)(2,1)}, bf16[432,768]{1,0:T(8,128)(2,1)}, bf16[36,144...) custom-call(f32[432,768]{1,0:T(8,128)} %get-tuple-element.63.tot_ref, ...), custom_call_target="tpu_custom_call" | custom-call | flops 2038431744 | bytes 11867136 | tf_op jit(solution)/shard_map/self_forward/pallas_call | solution.py:357
  144.1 49.9 %all-gather.15.cloned.1.call-done.m_ref = bf16[2,768,3072]{2,1,0:T(8,128)(2,1)} async-done(((bf16[2,96,3072]{2,1,0:T(8,128)(2,1)}), bf16[2,768,3072]{2,1,0:T(8,128)(2,1)}) %all-gather.15.cloned.1.call-update) | async-done | bytes 9437200 | tf_op jit(solution)/shard_map/all_gather | solution.py:472
  193.9 30.7 %feed.3 = (bf16[432,768]{1,0:T(8,128)(2,1)}, f32[432,768]{1,0:T(8,128)}, bf16[768,3072]{1,0:T(8,128)(2,1)}, bf16[768,3072]{1,0:T(8,128)(2,1)}, f32[32,768]{1,0:T(8,128)}) custom-call(s32[1]{0:T(128)} %bitcast.me_ref, f32[432,768]{1,0:T(8,128)} %get-tuple-element.64.tot_ref, bf16[432,768]{1,0:T(8,128)(2,1)} %reshape.244.cot_ref, ...), custom_call_target="tpu_custom_call" | custom-call | flops 12230590464 | bytes 23052292 | tf_op jit(solution)/shard_map/feed/pallas_call | solution.py:357
  224.6 19.7 %self_backward.3 = (f32[432,768]{1,0:T(8,128)}, bf16[1536,768]{1,0:T(8,128)(2,1)}, bf16[1536,768]{1,0:T(8,128)(2,1)}, f32[32,768]{1,0:T(8,128)}) custom-call(s32[1]{0:T(128)} %bitcast.me_ref, f32[432,768]{1,0:T(8,128)} %get-tuple-element.73.dtot_ref, f32[432,768]{1,0:T(8,128)} %get-tuple-element.63.tot_ref, ...), custom_call_target="tpu_custom_call" | custom-call | flops 4076863488 | bytes 17762308 | tf_op jit(solution)/shard_map/self_backward/pallas_call | solution.py:357
  244.6 10.0 %all-gather.11.cloned.1.call-done.m_ref = bf16[2,768,3072]{2,1,0:T(8,128)(2,1)} async-done(((bf16[2,96,3072]{2,1,0:T(8,128)(2,1)}), bf16[2,768,3072]{2,1,0:T(8,128)(2,1)}) %all-gather.11.cloned.1.call-update) | async-done | bytes 9437200 | tf_op jit(solution)/shard_map/all_gather | solution.py:472
  254.6 22.4 %feed.2 = (bf16[240,768]{1,0:T(8,128)(2,1)}, f32[240,768]{1,0:T(8,128)}, bf16[768,3072]{1,0:T(8,128)(2,1)}, bf16[768,3072]{1,0:T(8,128)(2,1)}, f32[32,768]{1,0:T(8,128)}) custom-call(s32[1]{0:T(128)} %bitcast.me_ref, f32[240,768]{1,0:T(8,128)} %get-tuple-element.61.tot_ref, bf16[240,768]{1,0:T(8,128)(2,1)} %reshape.242.cot_ref, ...), custom_call_target="tpu_custom_call" | custom-call | flops 6794772480 | bytes 21282820 | tf_op jit(solution)/shard_map/feed/pallas_call | solution.py:357
  277.0 13.9 %self_backward.2 = (f32[240,768]{1,0:T(8,128)}, bf16[1536,768]{1,0:T(8,128)(2,1)}, bf16[1536,768]{1,0:T(8,128)(2,1)}, f32[32,768]{1,0:T(8,128)}) custom-call(s32[1]{0:T(128)} %bitcast.me_ref, f32[240,768]{1,0:T(8,128)} %get-tuple-element.66.dtot_ref, f32[240,768]{1,0:T(8,128)} %get-tuple-element.60.tot_ref, ...), custom_call_target="tpu_custom_call" | custom-call | flops 2264924160 | bytes 13780996 | tf_op jit(solution)/shard_map/self_backward/pallas_call | solution.py:357
  291.2 28.4 %cross_backward.1 = (bf16[240,768]{1,0:T(8,128)(2,1)}, bf16[432,768]{1,0:T(8,128)(2,1)}, bf16[1664,768]{1,0:T(8,128)(2,1)}, bf16[1664,768]{1,0:T(8,128)(2,1)}) custom-call(s32[1]{0:T(128)} %bitcast.me_ref, f32[240,768]{1,0:T(8,128)} %get-tuple-element.72.dw_ref, f32[432,768]{1,0:T(8,128)} %get-tuple-element.79.dr_ref, bf16[240,768]{1,0:T(8,128)(2,1)} %reshape.240.words_ref, ...), custom_call_target="tpu_custom_call" | custom-call | flops 6341787648 | bytes 20140036 | tf_op jit(solution)/shard_map/cross_backward/pallas_call | solution.py:357
  329.3 9.6 %collective-permute-done.13 = bf16[384,768]{1,0:T(8,128)(2,1)S(1)} collective-permute-done((bf16[384,768]{1,0:T(8,128)(2,1)S(1)}, bf16[384,768]{1,0:T(8,128)(2,1)S(1)}, u32[]{:S(2)}, u32[]{:S(2)}) %collective-permute-start.13) | collective-permute-done | bytes 589856 | tf_op jit(solution)/shard_map/ppermute | solution.py:429
  341.1 10.4 %collective-permute-done.8 = bf16[384,768]{1,0:T(8,128)(2,1)S(1)} collective-permute-done((bf16[384,768]{1,0:T(8,128)(2,1)S(1)}, bf16[384,768]{1,0:T(8,128)(2,1)S(1)}, u32[]{:S(2)}, u32[]{:S(2)}) %collective-permute-start.8) | collective-permute-done | bytes 589856 | tf_op jit(solution)/shard_map/ppermute | solution.py:429
  354.4 9.1 %collective-permute-done.3 = bf16[384,768]{1,0:T(8,128)(2,1)S(1)} collective-permute-done((bf16[384,768]{1,0:T(8,128)(2,1)S(1)}, bf16[384,768]{1,0:T(8,128)(2,1)S(1)}, u32[]{:S(2)}, u32[]{:S(2)}) %collective-permute-start.3) | collective-permute-done | bytes 589856 | tf_op jit(solution)/shard_map/ppermute | solution.py:429
  364.6 9.4 %collective-permute-done.14 = bf16[192,768]{1,0:T(8,128)(2,1)S(1)} collective-permute-done((bf16[192,768]{1,0:T(8,128)(2,1)S(1)}, bf16[192,768]{1,0:T(8,128)(2,1)S(1)}, u32[]{:S(2)}, u32[]{:S(2)}) %collective-permute-start.14) | collective-permute-done | bytes 294944 | tf_op jit(solution)/shard_map/ppermute | solution.py:429
  398.4 17.6 %collective-permute-done.21 = bf16[192,3072]{1,0:T(8,128)(2,1)S(1)} collective-permute-done((bf16[192,3072]{1,0:T(8,128)(2,1)S(1)}, bf16[192,3072]{1,0:T(8,128)(2,1)S(1)}, u32[]{:S(2)}, u32[]{:S(2)}) %collective-permute-start.21) | collective-permute-done | bytes 1179680 | tf_op jit(solution)/shard_map/ppermute | solution.py:429
  417.7 5.2 collective-permute-done.23
  423.4 17.9 %collective-permute-done.16 = bf16[192,3072]{1,0:T(8,128)(2,1)S(1)} collective-permute-done((bf16[192,3072]{1,0:T(8,128)(2,1)S(1)}, bf16[192,3072]{1,0:T(8,128)(2,1)S(1)}, u32[]{:S(2)}, u32[]{:S(2)}) %collective-permute-start.16) | collective-permute-done | bytes 1179680 | tf_op jit(solution)/shard_map/ppermute | solution.py:429
  448.7 12.2 %collective-permute-done.22 = bf16[96,3072]{1,0:T(8,128)(2,1)S(1)} collective-permute-done((bf16[96,3072]{1,0:T(8,128)(2,1)S(1)}, bf16[96,3072]{1,0:T(8,128)(2,1)S(1)}, u32[]{:S(2)}, u32[]{:S(2)}) %collective-permute-start.22) | collective-permute-done | bytes 589856 | tf_op jit(solution)/shard_map/ppermute | solution.py:429
  474.5 12.9 %psum.79 = bf16[32,96]{1,0:T(8,128)(2,1)S(1)} all-reduce(bf16[32,96]{1,0:T(8,128)(2,1)S(1)} %slice.413), channel_id=1, replica_groups=mesh['dp'=4,'fsdp'=8] {'dp'}, use_global_device_ids=true, to_apply=%region_2.3 | all-reduce | flops 3072 | bytes 12288 | tf_op jit(solution)/shard_map/psum | solution.py:544
  488.6 137.4 %all-reduce.4.cloned.1.call-done = (bf16[192,768]{1,0:T(8,128)(2,1)}, bf16[192,768]{1,0:T(8,128)(2,1)}, bf16[192,768]{1,0:T(8,128)(2,1)}, bf16[192,768]{1,0:T(8,...) async-done(((bf16[192,768]{1,0:T(8,128)(2,1)}, ...) | async-done | bytes 4128784 | tf_op jit(solution)/shard_map/psum | solution.py:544
  (183 shorter events, 85.7 us)
Async XLA Ops:
  7.2 44.4 %all-gather.7.cloned.1.call-start = ((), (), s32[]{:S(2)}) async-start(), calls=%async_computation | async-start | bytes 5308416 | tf_op jit(solution)/shard_map/all_gather | solution.py:472
  7.9 84.5 %all-gather.9.cloned.1.call-start = ((), (), s32[]{:S(2)}) async-start(), calls=%async_computation.1 | async-start | bytes 5308416 | tf_op jit(solution)/shard_map/all_gather | solution.py:472
  8.7 124.6 %all-gather.13.cloned.1.call-start = ((), (), s32[]{:S(2)}) async-start(), calls=%async_computation.3 | async-start | bytes 5308416 | tf_op jit(solution)/shard_map/all_gather | solution.py:472
  9.5 184.5 %all-gather.15.cloned.1.call-start = ((), (), s32[]{:S(2)}) async-start(), calls=%async_computation.4 | async-start | bytes 10616832 | tf_op jit(solution)/shard_map/all_gather | solution.py:472
  10.1 244.5 %all-gather.11.cloned.1.call-start = ((), (), s32[]{:S(2)}) async-start(), calls=%async_computation.2 | async-start | bytes 10616832 | tf_op jit(solution)/shard_map/all_gather | solution.py:472
  10.7 615.3 %all-reduce.4.cloned.1.call-start = ((), (), s32[]{:S(2)}) async-start(), calls=%async_computation.5 | async-start | bytes 8257536 | tf_op jit(solution)/shard_map/psum | solution.py:544
  244.3 76.0 %collective-permute-start.10 = (bf16[1536,768]{1,0:T(8,128)(2,1)}, bf16[1536,768]{1,0:T(8,128)(2,1)}, u32[]{:S(2)}, u32[]{:S(2)}) collective-permute-start(bf16[1536,768]{1,0:T(8,128)(2,1)} %get-tuple-element.101), channel_id=1, source_target_pairs={{0,1},{1,0},{2,3},{3,2},{4,5},{5,4},{6,7},{7,6},{8,9},{9,8},{10,11... | collective-permute-start | bytes 7077896 | tf_op jit(solution)/shard_map/ppermute | solution.py:429
  290.9 32.8 %collective-permute-start.5 = (bf16[1536,768]{1,0:T(8,128)(2,1)}, bf16[1536,768]{1,0:T(8,128)(2,1)}, u32[]{:S(2)}, u32[]{:S(2)}) collective-permute-start(bf16[1536,768]{1,0:T(8,128)(2,1)} %get-tuple-element.99), channel_id=1, source_target_pairs={{0,1},{1,0},{2,3},{3,2},{4,5},{5,4},{6,7},{7,6},{8,9},{9,8},{10,11... | collective-permute-start | bytes 7077896 | tf_op jit(solution)/shard_map/ppermute | solution.py:429
  319.8 65.4 %collective-permute-start.20 = (bf16[768,3072]{1,0:T(8,128)(2,1)}, bf16[768,3072]{1,0:T(8,128)(2,1)S(1)}, u32[]{:S(2)}, u32[]{:S(2)}) collective-permute-start(bf16[768,3072]{1,0:T(8,128)(2,1)} %get-tuple-element.105), channel_id=1, source_target_pairs={{0,1},{1,0},{2,3},{3,2},{4,5},{5,4},{6,7},{7,6},{8,9},{9,8},{10,11... | collective-permute-start | bytes 14155784 | tf_op jit(solution)/shard_map/ppermute | solution.py:429
  320.0 74.6 %collective-permute-start.15 = (bf16[768,3072]{1,0:T(8,128)(2,1)}, bf16[768,3072]{1,0:T(8,128)(2,1)S(1)}, u32[]{:S(2)}, u32[]{:S(2)}) collective-permute-start(bf16[768,3072]{1,0:T(8,128)(2,1)} %get-tuple-element.103), channel_id=1, source_target_pairs={{0,1},{1,0},{2,3},{3,2},{4,5},{5,4},{6,7},{7,6},{8,9},{9,8},{10,11... | collective-permute-start | bytes 14155784 | tf_op jit(solution)/shard_map/ppermute | solution.py:429
  322.6 16.2 %collective-permute-start.13 = (bf16[384,768]{1,0:T(8,128)(2,1)S(1)}, bf16[384,768]{1,0:T(8,128)(2,1)S(1)}, u32[]{:S(2)}, u32[]{:S(2)}) collective-permute-start(bf16[384,768]{1,0:T(8,128)(2,1)S(1)} %get-tuple-element.129), channel_id=1, source_target_pairs={{0,4},{1,5},{2,6},{3,7},{4,0},{5,1},{6,2},{7,3},{8,12},{9,13},{10,... | collective-permute-start | bytes 1769480 | tf_op jit(solution)/shard_map/ppermute | solution.py:429
  323.7 16.6 %collective-permute-start.11 = (bf16[384,768]{1,0:T(8,128)(2,1)S(1)}, bf16[384,768]{1,0:T(8,128)(2,1)S(1)}, u32[]{:S(2)}, u32[]{:S(2)}) collective-permute-start(bf16[384,768]{1,0:T(8,128)(2,1)S(1)} %get-tuple-element.130), channel_id=1, source_target_pairs={{0,2},{1,3},{2,0},{3,1},{4,6},{5,7},{6,4},{7,5},{8,10},{9,11},{10,... | collective-permute-start | bytes 1769480 | tf_op jit(solution)/shard_map/ppermute | solution.py:429
  327.1 24.4 %collective-permute-start.8 = (bf16[384,768]{1,0:T(8,128)(2,1)S(1)}, bf16[384,768]{1,0:T(8,128)(2,1)S(1)}, u32[]{:S(2)}, u32[]{:S(2)}) collective-permute-start(bf16[384,768]{1,0:T(8,128)(2,1)S(1)} %get-tuple-element.133), channel_id=1, source_target_pairs={{0,4},{1,5},{2,6},{3,7},{4,0},{5,1},{6,2},{7,3},{8,12},{9,13},{10,... | collective-permute-start | bytes 1769480 | tf_op jit(solution)/shard_map/ppermute | solution.py:429
  340.4 23.1 %collective-permute-start.3 = (bf16[384,768]{1,0:T(8,128)(2,1)S(1)}, bf16[384,768]{1,0:T(8,128)(2,1)S(1)}, u32[]{:S(2)}, u32[]{:S(2)}) collective-permute-start(bf16[384,768]{1,0:T(8,128)(2,1)S(1)} %get-tuple-element.125), channel_id=1, source_target_pairs={{0,4},{1,5},{2,6},{3,7},{4,0},{5,1},{6,2},{7,3},{8,12},{9,13},{10,... | collective-permute-start | bytes 1769480 | tf_op jit(solution)/shard_map/ppermute | solution.py:429
  351.5 33.0 %collective-permute-start.1 = (bf16[448,768]{1,0:T(8,128)(2,1)S(1)}, bf16[448,768]{1,0:T(8,128)(2,1)S(1)}, u32[]{:S(2)}, u32[]{:S(2)}) collective-permute-start(bf16[448,768]{1,0:T(8,128)(2,1)S(1)} %get-tuple-element.127), channel_id=1, source_target_pairs={{0,2},{1,3},{2,0},{3,1},{4,6},{5,7},{6,4},{7,5},{8,10},{9,11},{10,... | collective-permute-start | bytes 2064392 | tf_op jit(solution)/shard_map/ppermute | solution.py:429
  353.0 20.9 %collective-permute-start.14 = (bf16[192,768]{1,0:T(8,128)(2,1)S(1)}, bf16[192,768]{1,0:T(8,128)(2,1)S(1)}, u32[]{:S(2)}, u32[]{:S(2)}) collective-permute-start(bf16[192,768]{1,0:T(8,128)(2,1)S(1)} %add_convert_fusion.36), channel_id=1, source_target_pairs={{0,2},{1,3},{2,0},{3,1},{4,6},{5,7},{6,4},{7,5},{8,10},{9,11},{10,... | collective-permute-start | bytes 884744 | tf_op jit(solution)/shard_map/ppermute | solution.py:429
  387.1 29.0 %collective-permute-start.21 = (bf16[192,3072]{1,0:T(8,128)(2,1)S(1)}, bf16[192,3072]{1,0:T(8,128)(2,1)S(1)}, u32[]{:S(2)}, u32[]{:S(2)}) collective-permute-start(bf16[192,3072]{1,0:T(8,128)(2,1)S(1)} %get-tuple-element.119), channel_id=1, source_target_pairs={{0,2},{1,3},{2,0},{3,1},{4,6},{5,7},{6,4},{7,5},{8,10},{9,11},{10,... | collective-permute-start | bytes 3538952 | tf_op jit(solution)/shard_map/ppermute | solution.py:429
  394.1 28.9 %collective-permute-start.23 = (bf16[192,3072]{1,0:T(8,128)(2,1)S(1)}, bf16[192,3072]{1,0:T(8,128)(2,1)S(1)}, u32[]{:S(2)}, u32[]{:S(2)}) collective-permute-start(bf16[192,3072]{1,0:T(8,128)(2,1)S(1)} %get-tuple-element.117), channel_id=1, source_target_pairs={{0,4},{1,5},{2,6},{3,7},{4,0},{5,1},{6,2},{7,3},{8,12},{9,13},{10,... | collective-permute-start | bytes 3538952 | tf_op jit(solution)/shard_map/ppermute | solution.py:429
  396.7 44.7 %collective-permute-start.16 = (bf16[192,3072]{1,0:T(8,128)(2,1)S(1)}, bf16[192,3072]{1,0:T(8,128)(2,1)S(1)}, u32[]{:S(2)}, u32[]{:S(2)}) collective-permute-start(bf16[192,3072]{1,0:T(8,128)(2,1)S(1)} %get-tuple-element.123), channel_id=1, source_target_pairs={{0,2},{1,3},{2,0},{3,1},{4,6},{5,7},{6,4},{7,5},{8,10},{9,11},{10,... | collective-permute-start | bytes 3538952 | tf_op jit(solution)/shard_map/ppermute | solution.py:429
  397.8 50.5 %collective-permute-start.18 = (bf16[192,3072]{1,0:T(8,128)(2,1)S(1)}, bf16[192,3072]{1,0:T(8,128)(2,1)S(1)}, u32[]{:S(2)}, u32[]{:S(2)}) collective-permute-start(bf16[192,3072]{1,0:T(8,128)(2,1)S(1)} %get-tuple-element.121), channel_id=1, source_target_pairs={{0,4},{1,5},{2,6},{3,7},{4,0},{5,1},{6,2},{7,3},{8,12},{9,13},{10,... | collective-permute-start | bytes 3538952 | tf_op jit(solution)/shard_map/ppermute | solution.py:429
  416.2 44.7 %collective-permute-start.22 = (bf16[96,3072]{1,0:T(8,128)(2,1)S(1)}, bf16[96,3072]{1,0:T(8,128)(2,1)S(1)}, u32[]{:S(2)}, u32[]{:S(2)}) collective-permute-start(bf16[96,3072]{1,0:T(8,128)(2,1)S(1)} %add_convert_fusion.14), channel_id=1, source_target_pairs={{0,4},{1,5},{2,6},{3,7},{4,0},{5,1},{6,2},{7,3},{8,12},{9,13},{10,... | collective-permute-start | bytes 1769480 | tf_op jit(solution)/shard_map/ppermute | solution.py:429
  423.1 38.8 %collective-permute-start.24 = (bf16[96,3072]{1,0:T(8,128)(2,1)S(1)}, bf16[96,3072]{1,0:T(8,128)(2,1)S(1)}, u32[]{:S(2)}, u32[]{:S(2)}) collective-permute-start(bf16[96,3072]{1,0:T(8,128)(2,1)S(1)} %add_convert_fusion.11), channel_id=1, source_target_pairs={{0,2},{1,3},{2,0},{3,1},{4,6},{5,7},{6,4},{7,5},{8,10},{9,11},{10,... | collective-permute-start | bytes 1769480 | tf_op jit(solution)/shard_map/ppermute | solution.py:429
  441.5 26.2 %collective-permute-start.17 = (bf16[96,3072]{1,0:T(8,128)(2,1)S(1)}, bf16[96,3072]{1,0:T(8,128)(2,1)S(1)}, u32[]{:S(2)}, u32[]{:S(2)}) collective-permute-start(bf16[96,3072]{1,0:T(8,128)(2,1)S(1)} %add_convert_fusion.20), channel_id=1, source_target_pairs={{0,4},{1,5},{2,6},{3,7},{4,0},{5,1},{6,2},{7,3},{8,12},{9,13},{10,... | collective-permute-start | bytes 1769480 | tf_op jit(solution)/shard_map/ppermute | solution.py:429
  448.4 20.4 %collective-permute-start.19 = (bf16[96,3072]{1,0:T(8,128)(2,1)S(1)}, bf16[96,3072]{1,0:T(8,128)(2,1)S(1)}, u32[]{:S(2)}, u32[]{:S(2)}) collective-permute-start(bf16[96,3072]{1,0:T(8,128)(2,1)S(1)} %add_convert_fusion.17), channel_id=1, source_target_pairs={{0,2},{1,3},{2,0},{3,1},{4,6},{5,7},{6,4},{7,5},{8,10},{9,11},{10,... | collective-permute-start | bytes 1769480 | tf_op jit(solution)/shard_map/ppermute | solution.py:429
  (37 other events, 306.6 us)
Sparse Core Ops, SparseCore 0:
  9.9 41.6 all-gather.6
  53.5 38.9 all-gather.8
  94.4 38.9 all-gather.12
  135.1 58.8 all-gather.14
  195.7 58.8 all-gather.10
  469.9 156.0 all-reduce.3
